TPU v7x, 256 devices: a whole 4x4x8 slice. The times are simulated.
256 devices in a mesh: grp: 8 (over z), seq: 32 (over x, y, core).
Axes of the slice: x: 4, y: 4, z: 8, core: 2. Of those that a mesh axis runs over, the one named last changes fastest.
Arguments:
- queries: bfloat16 [8, 1024, 4096], P('grp', 'seq'), may hold values from -96 to 96
- attn_keys: bfloat16 [8, 1024, 4096], P('grp', 'seq'), may hold values from -4 to 4
- attn_values: bfloat16 [8, 1024, 4096], P('grp', 'seq'), may hold values from -6 to 6
- byte_grads: bfloat16 [8, 8192, 4096], P('grp', 'seq'), may hold values from -6 to 6
- seg_starts: int32 [8, 32, 32], P('grp', 'seq'), may hold values from 0 to 256, as said below
- up_gain: float32 [4096], replicated, may hold values from 0.1 to 1.9
Outputs:
- grad_queries: bfloat16 [8, 1024, 4096], P('grp', 'seq')
- grad_keys: bfloat16 [8, 1024, 4096], P('grp', 'seq')
- grad_values: bfloat16 [8, 1024, 4096], P('grp', 'seq')
- grad_gain: float32 [4096], P('seq')
Inputs may be any that keep to these rules, and one draw needn't show every extreme that they name: `seg_starts`: in every row each shard's entries rise strictly, the used ones below 256 and the unused slots after them equal to 256; every shard starts at least 8 segments and some shard of every row exactly 32; shard 0's first entry is 0.
All inputs are finite; a program needn't handle non-finite values.
Results may differ from a plain program's by a relative error of at most 0.012.
Values may be sent and summed in bfloat16 or wider, within the bound.
No kernel may reach another device: no remote copies, remote signals or barrier semaphores. Data moves between devices by JAX's collectives and lax.ppermute only.
A program may use at most 64 MiB of HBM per device.

v0:
```python
import math
import jax
import jax.numpy as jnp
from jax import lax
from jax.sharding import PartitionSpec as P

HD = 128


def shifted(value, axis, by):
    devices = lax.axis_size(axis)
    pairs = [(i, i + by) for i in range(devices) if 0 <= i + by < devices]
    return lax.ppermute(value, axis, pairs)


def shortened(value):
    return jax.tree.map(lambda a: a.astype(jnp.bfloat16) if a.dtype == jnp.float32 else a, value)


def head_grads(query_head, key_head, value_head, upstream, key_valid):
    seq_rows = query_head.shape[0]
    head_width = query_head.shape[1]
    block_rows = math.gcd(seq_rows, 512)
    block_total = seq_rows // block_rows
    scaling = 1.0 / math.sqrt(head_width)
    key_total = jnp.zeros((seq_rows, head_width), jnp.float32)
    value_total = jnp.zeros((seq_rows, head_width), jnp.float32)
    query_parts = []
    output_parts = []
    for block_index in range(block_total):
        first_row = block_index * block_rows
        prefix = first_row + block_rows
        query_block = query_head[first_row:prefix]
        upstream_block = upstream[first_row:prefix]
        key_prefix = key_head[:prefix]
        value_prefix = value_head[:prefix]
        scores = (
            jnp.einsum("qd,kd->qk", query_block, key_prefix, preferred_element_type=jnp.float32)
            * scaling
        )
        row_ids = first_row + jnp.arange(block_rows, dtype=jnp.int32)[:, None]
        col_ids = jnp.arange(prefix, dtype=jnp.int32)[None, :]
        allowed = (col_ids <= row_ids) & key_valid[None, :prefix]
        scores = jnp.where(allowed, scores, -1e30)
        row_max = jnp.max(scores, axis=1, keepdims=True)
        weights = jnp.exp(scores - row_max)
        attn_probs = weights / jnp.sum(weights, axis=1, keepdims=True)
        probs_low = attn_probs.astype(jnp.bfloat16)
        attn_out = jnp.einsum(
            "qk,kd->qd", probs_low, value_prefix, preferred_element_type=jnp.float32
        ).astype(jnp.bfloat16)
        grad_probs = jnp.einsum(
            "qd,kd->qk", upstream_block, value_prefix, preferred_element_type=jnp.float32
        )
        row_delta = jnp.sum(
            upstream_block.astype(jnp.float32) * attn_out.astype(jnp.float32), axis=1, keepdims=True
        )
        grad_scores = (attn_probs * (grad_probs - row_delta)).astype(jnp.bfloat16)
        grad_query = (
            jnp.einsum("qk,kd->qd", grad_scores, key_prefix, preferred_element_type=jnp.float32)
            * scaling
        ).astype(jnp.bfloat16)
        key_total = key_total.at[:prefix].add(
            jnp.einsum("qk,qd->kd", grad_scores, query_block, preferred_element_type=jnp.float32)
        )
        value_total = value_total.at[:prefix].add(
            jnp.einsum("qk,qd->kd", probs_low, upstream_block, preferred_element_type=jnp.float32)
        )
        query_parts.append(grad_query)
        output_parts.append(attn_out)
    grad_query = jnp.concatenate(query_parts, axis=0)
    attn_out = jnp.concatenate(output_parts, axis=0)
    grad_key = (key_total * scaling).astype(jnp.bfloat16)
    grad_value = value_total.astype(jnp.bfloat16)
    return (grad_query, grad_key, grad_value, attn_out)


def pool_bytes(byte_grads, seg_starts, slot_count):
    byte_count = byte_grads.shape[1]
    local_starts = seg_starts[0, 0]
    filled = jnp.sum((local_starts < byte_count).astype(jnp.int32))
    position = jnp.arange(byte_count, dtype=jnp.int32)
    started = jnp.sum((local_starts[None, :] <= position[:, None]).astype(jnp.int32), axis=1)
    slot_ids = jnp.arange(slot_count, dtype=jnp.int32)
    member = (started[None, :] - 1 == slot_ids[:, None]).astype(jnp.bfloat16)
    byte_rows = byte_grads[0]
    own_sums = jnp.dot(member, byte_rows, preferred_element_type=jnp.float32)
    leading = (started == 0).astype(jnp.bfloat16)[None, :]
    carried = jnp.dot(leading, byte_rows, preferred_element_type=jnp.float32)
    incoming = shifted(carried, "seq", -1)
    is_last = (slot_ids == filled - 1)[:, None]
    pooled = own_sums + jnp.where(is_last, incoming, 0.0)
    return pooled.astype(jnp.bfloat16)


def per_device(queries, attn_keys, attn_values, byte_grads, seg_starts, up_gain):
    slot_count = queries.shape[1]
    model_width = queries.shape[2]
    byte_count = byte_grads.shape[1]
    seq_count = lax.axis_size("seq")
    shard_index = lax.axis_index("seq")
    heads_here = model_width // (seq_count * HD)
    col_count = heads_here * HD
    all_starts = lax.all_gather(seg_starts[0], "seq", axis=0, tiled=True)
    key_valid = (all_starts < byte_count).reshape(-1)

    def by_heads(tensor):
        return tensor.reshape(slot_count, seq_count * heads_here, HD)

    pooled_low = pool_bytes(byte_grads, seg_starts, slot_count)
    head_query, head_key, head_value, head_pool = (
        lax.all_to_all(by_heads(queries[0]), "seq", split_axis=1, concat_axis=0, tiled=True),
        lax.all_to_all(by_heads(attn_keys[0]), "seq", split_axis=1, concat_axis=0, tiled=True),
        lax.all_to_all(by_heads(attn_values[0]), "seq", split_axis=1, concat_axis=0, tiled=True),
        lax.all_to_all(by_heads(pooled_low), "seq", split_axis=1, concat_axis=0, tiled=True),
    )
    gain_here = lax.dynamic_slice_in_dim(up_gain, shard_index * col_count, col_count).reshape(
        1, heads_here, HD
    )
    upstream = (gain_here * head_pool.astype(jnp.float32)).astype(jnp.bfloat16)

    def per_head(head_items):
        return head_grads(head_items[0], head_items[1], head_items[2], head_items[3], key_valid)

    stacked = tuple(
        (jnp.moveaxis(operand, 1, 0) for operand in (head_query, head_key, head_value, upstream))
    )
    results = lax.map(per_head, stacked)
    grad_query, grad_key, grad_value, attn_out = tuple(
        (jnp.moveaxis(operand, 0, 1) for operand in results)
    )

    def to_seq(tensor):
        return tensor.reshape(1, slot_count, model_width)

    returned = (
        lax.all_to_all(
            shortened(grad_query), "seq", split_axis=0, concat_axis=1, tiled=True
        ).astype(grad_query.dtype),
        lax.all_to_all(grad_key, "seq", split_axis=0, concat_axis=1, tiled=True),
        lax.all_to_all(grad_value, "seq", split_axis=0, concat_axis=1, tiled=True),
        lax.all_to_all(shortened(attn_out), "seq", split_axis=0, concat_axis=1, tiled=True).astype(
            attn_out.dtype
        ),
    )
    seq_out = returned[3].reshape(slot_count, model_width)
    seq_terms = jnp.sum(seq_out.astype(jnp.float32) * pooled_low.astype(jnp.float32), axis=0)
    gain_total = lax.psum(seq_terms, ("grp", "seq"))
    grad_gain = lax.dynamic_slice_in_dim(gain_total, shard_index * col_count, col_count)
    return (to_seq(returned[0]), to_seq(returned[1]), to_seq(returned[2]), grad_gain)


def solution(mesh):
    return jax.shard_map(
        per_device,
        mesh=mesh,
        in_specs=(
            P("grp", "seq", None),
            P("grp", "seq", None),
            P("grp", "seq", None),
            P("grp", "seq", None),
            P("grp", "seq", None),
            P(),
        ),
        out_specs=(P("grp", "seq", None), P("grp", "seq", None), P("grp", "seq", None), P("seq")),
        check_vma=False,
    )
```

profile of v0, /device:TPU:1, one launch (start us, length us, event | category | flops | bytes accessed | tf_op | source)
XLA Modules:
  0.0 227.1 jit_solution(2610333382745810122)
XLA Ops:
  0.7 1.1 copy.88
  1.8 0.8 copy.70
  2.6 8.6 %all-to-all-start = ((bf16[32,32,128]{2,0,1:T(8,128)(2,1)}), bf16[32,32,128]{2,0,1:T(8,128)(2,1)S(1)}, u32[]{:S(2)}, u32[]{:S(2)}) async-start(bf16[32,32,128]{2,0,1:T(8,128)(2,1)} %copy.70), calls=%async_computation | async-start | bytes 524288 | tf_op jit(solution)/shard_map/all_to_all | solution.py:112
  11.2 0.7 convert_reduce_fusion
  12.4 2.1 collective-permute-start
  14.5 23.7 %all-gather = s32[32,1,32]{2,1,0:T(1,128)S(1)} all-gather(s32[1,1,32]{2,1,0:T(1,128)S(1)} %copy-done.19), channel_id=2, replica_groups=mesh['grp'=8,'seq'=32] {'seq'}, dimensions={0}, use_global_device_ids=true | all-gather | bytes 4224 | tf_op jit(solution)/shard_map/all_gather | solution.py:104
  39.7 0.8 copy.71
  40.7 0.8 copy.73
  41.5 0.8 dynamic_slice.15
  42.8 5.8 %all-to-all-start.1 = ((bf16[32,32,128]{2,0,1:T(8,128)(2,1)}), bf16[32,32,128]{2,0,1:T(8,128)(2,1)S(1)}, u32[]{:S(2)}, u32[]{:S(2)}) async-start(bf16[32,32,128]{2,0,1:T(8,128)(2,1)} %copy.71), calls=%async_computation.1 | async-start | bytes 524288 | tf_op jit(solution)/shard_map/all_to_all | solution.py:113
  48.5 0.7 copy_bitcast_fusion
  49.3 8.2 %all-to-all-done.1 = bf16[32,32,128]{2,0,1:T(8,128)(2,1)S(1)} async-done(((bf16[32,32,128]{2,0,1:T(8,128)(2,1)}), bf16[32,32,128]{2,0,1:T(8,128)(2,1)S(1)}, u32[]{:S(2)}, u32[]{:S(2)}) %all-to-all-start.1) | async-done | bytes 262176 | tf_op jit(solution)/shard_map/all_to_all | solution.py:113
  57.5 3.7 %all-to-all-start.3 = ((bf16[32,32,128]{2,0,1:T(8,128)(2,1)}), bf16[32,32,128]{2,0,1:T(8,128)(2,1)S(1)}, u32[]{:S(2)}, u32[]{:S(2)}) async-start(bf16[32,32,128]{2,0,1:T(8,128)(2,1)} %copy.73), calls=%async_computation.3 | async-start | bytes 524288 | tf_op jit(solution)/shard_map/all_to_all | solution.py:114
  61.9 0.8 fusion.32
  63.2 1.8 fusion.5
  65.0 5.4 %all-to-all-done.3 = bf16[32,32,128]{2,0,1:T(8,128)(2,1)S(1)} async-done(((bf16[32,32,128]{2,0,1:T(8,128)(2,1)}), bf16[32,32,128]{2,0,1:T(8,128)(2,1)S(1)}, u32[]{:S(2)}, u32[]{:S(2)}) %all-to-all-start.3) | async-done | bytes 262176 | tf_op jit(solution)/shard_map/all_to_all | solution.py:114
  70.4 4.4 %all-to-all-start.2 = ((bf16[32,32,128]{2,0,1:T(8,128)(2,1)}), bf16[32,32,128]{2,0,1:T(8,128)(2,1)}, u32[]{:S(2)}, u32[]{:S(2)}) async-start(bf16[32,32,128]{2,0,1:T(8,128)(2,1)} %copy_bitcast_fusion), calls=%async_computation.2 | async-start | bytes 524288 | tf_op jit(solution)/shard_map/all_to_all | solution.py:115
  75.4 1.3 fusion.33
  76.9 1.1 convolution_convert_fusion.1
  78.0 1.0 fusion.24
  78.9 4.9 %all-to-all-done.2 = bf16[32,32,128]{2,0,1:T(8,128)(2,1)} async-done(((bf16[32,32,128]{2,0,1:T(8,128)(2,1)}), bf16[32,32,128]{2,0,1:T(8,128)(2,1)}, u32[]{:S(2)}, u32[]{:S(2)}) %all-to-all-start.2) | async-done | bytes 262176 | tf_op jit(solution)/shard_map/all_to_all | solution.py:115
  83.9 1.0 bitcast_convert_fusion
  85.0 2.2 multiply_reduce_fusion.1
  89.5 1.1 fusion.16
  91.6 0.8 reduce.17
  92.4 0.8 reshape.259
  93.2 3.7 %all-to-all-start.5 = ((bf16[32,2,2048]{2,1,0:T(2,128)(2,1)}), bf16[32,2,2048]{2,1,0:T(2,128)(2,1)S(1)}, u32[]{:S(2)}, u32[]{:S(2)}) async-start(bf16[32,2,2048]{2,1,0:T(2,128)(2,1)} %reshape.259), calls=%async_computation.5 | async-start | bytes 524288 | tf_op jit(solution)/shard_map/all_to_all | solution.py:140
  97.3 1.0 maximum_bitcast_fusion
  98.3 1.5 reduce.16
  99.8 1.7 reshape.257
  101.5 4.5 %all-to-all-done.5 = bf16[32,2,2048]{2,1,0:T(2,128)(2,1)S(1)} async-done(((bf16[32,2,2048]{2,1,0:T(2,128)(2,1)}), bf16[32,2,2048]{2,1,0:T(2,128)(2,1)S(1)}, u32[]{:S(2)}, u32[]{:S(2)}) %all-to-all-start.5) | async-done | bytes 262176 | tf_op jit(solution)/shard_map/all_to_all | solution.py:140
  106.0 3.7 %all-to-all-start.4 = ((bf16[32,2,2048]{2,1,0:T(2,128)(2,1)}), bf16[32,2,2048]{2,1,0:T(2,128)(2,1)S(1)}, u32[]{:S(2)}, u32[]{:S(2)}) async-start(bf16[32,2,2048]{2,1,0:T(2,128)(2,1)} %reshape.257), calls=%async_computation.4 | async-start | bytes 524288 | tf_op jit(solution)/shard_map/all_to_all | solution.py:137
  109.7 1.6 maximum_bitcast_fusion.1
  111.4 2.4 %reduce.19 = bf16[1024,128]{1,0:T(8,128)(2,1)} reduce(bf16[1024,1,128]{2,0,1:T(8,128)(2,1)} %maximum_bitcast_fusion.1, bf16[]{:T(256)} %broadcast.160), dimensions={1}, to_apply=%copy.81.reduce_sub_computation | reduce | bytes 524290 | tf_op jit(solution)/shard_map/transpose | solution.py:130
  113.8 1.7 reshape.263
  115.5 3.3 %all-to-all-done.4 = bf16[32,2,2048]{2,1,0:T(2,128)(2,1)S(1)} async-done(((bf16[32,2,2048]{2,1,0:T(2,128)(2,1)}), bf16[32,2,2048]{2,1,0:T(2,128)(2,1)S(1)}, u32[]{:S(2)}, u32[]{:S(2)}) %all-to-all-start.4) | async-done | bytes 262176 | tf_op jit(solution)/shard_map/all_to_all | solution.py:137
  118.8 4.4 %all-to-all-start.7 = ((bf16[32,2,2048]{2,1,0:T(2,128)(2,1)}), bf16[32,2,2048]{2,1,0:T(2,128)(2,1)}, u32[]{:S(2)}, u32[]{:S(2)}) async-start(bf16[32,2,2048]{2,1,0:T(2,128)(2,1)} %reshape.263), calls=%async_computation.7 | async-start | bytes 524288 | tf_op jit(solution)/shard_map/all_to_all | solution.py:142
  123.5 2.1 fusion.14
  125.6 0.8 reduce.18
  126.4 0.8 reshape.261
  127.2 5.1 %all-to-all-done.7 = bf16[32,2,2048]{2,1,0:T(2,128)(2,1)} async-done(((bf16[32,2,2048]{2,1,0:T(2,128)(2,1)}), bf16[32,2,2048]{2,1,0:T(2,128)(2,1)}, u32[]{:S(2)}, u32[]{:S(2)}) %all-to-all-start.7) | async-done | bytes 262176 | tf_op jit(solution)/shard_map/all_to_all | solution.py:142
  132.3 4.6 %all-to-all-start.6 = ((bf16[32,2,2048]{2,1,0:T(2,128)(2,1)}), bf16[32,2,2048]{2,1,0:T(2,128)(2,1)}, u32[]{:S(2)}, u32[]{:S(2)}) async-start(bf16[32,2,2048]{2,1,0:T(2,128)(2,1)} %reshape.261), calls=%async_computation.6 | async-start | bytes 524288 | tf_op jit(solution)/shard_map/all_to_all | solution.py:141
  137.4 0.8 reshape.241
  138.6 0.8 reshape.240
  139.4 2.2 reshape.264
  142.8 80.6 %psum.7 = f32[4096]{0:T(1024)S(1)} all-reduce(f32[4096]{0:T(1024)S(1)} %fusion.20), channel_id=1, replica_groups=mesh['grp'=8,'seq'=32] {'grp','seq'}, use_global_device_ids=true, to_apply=%region_9.10 | all-reduce | flops 4096 | bytes 32768 | tf_op jit(solution)/shard_map/psum | solution.py:148
  224.0 2.2 reshape.262
  226.3 0.8 reshape.242
  (82 shorter events, 10.6 us)
Async XLA Ops:
  0.6 11.4 %copy-start = (bf16[1,256,4096]{2,1,0:T(8,128)(2,1)S(1)}, bf16[1,256,4096]{2,1,0:T(8,128)(2,1)}, u32[]{:S(2)}) copy-start(bf16[1,256,4096]{2,1,0:T(8,128)(2,1)} %param.21) | copy-start | bytes 6291460
  0.6 13.9 %copy-start.19 = (s32[1,1,32]{2,1,0:T(1,128)S(1)}, s32[1,1,32]{2,1,0:T(1,128)}, u32[]{:S(2)}) copy-start(s32[1,1,32]{2,1,0:T(1,128)} %param.22) | copy-start | bytes 388
  0.7 39.0 %copy-start.16 = (bf16[1,32,4096]{2,1,0:T(8,128)(2,1)S(1)}, bf16[1,32,4096]{2,1,0:T(8,128)(2,1)}, u32[]{:S(2)}) copy-start(bf16[1,32,4096]{2,1,0:T(8,128)(2,1)} %param.19) | copy-start | bytes 786436
  1.8 38.9 %copy-start.17 = (bf16[1,32,4096]{2,1,0:T(8,128)(2,1)S(1)}, bf16[1,32,4096]{2,1,0:T(8,128)(2,1)}, u32[]{:S(2)}) copy-start(bf16[1,32,4096]{2,1,0:T(8,128)(2,1)} %param.20) | copy-start | bytes 786436
  2.6 40.1 %all-to-all-start = ((bf16[32,32,128]{2,0,1:T(8,128)(2,1)}), bf16[32,32,128]{2,0,1:T(8,128)(2,1)S(1)}, u32[]{:S(2)}, u32[]{:S(2)}) async-start(bf16[32,32,128]{2,0,1:T(8,128)(2,1)} %copy.70), calls=%async_computation | async-start | bytes 524288 | tf_op jit(solution)/shard_map/all_to_all | solution.py:112
  12.4 29.9 %collective-permute-start = (f32[1,4096]{1,0:T(1,128)S(1)}, f32[1,4096]{1,0:T(1,128)S(1)}, u32[]{:S(2)}, u32[]{:S(2)}) collective-permute-start(f32[1,4096]{1,0:T(1,128)S(1)} %fusion), channel_id=1, source_target_pairs={{1,0},{2,1},{3,2},{4,3},{5,4},{6,5},{7,6},{8,7},{9,8},{10,9},{11,1... | collective-permute-start | bytes 49160 | tf_op jit(solution)/shard_map/ppermute | solution.py:13
  42.8 19.9 %copy-start.3 = (bf16[32,4096]{1,0:T(8,128)(2,1)}, bf16[32,4096]{1,0:T(8,128)(2,1)S(1)}, u32[]{:S(2)}) copy-start(bf16[32,4096]{1,0:T(8,128)(2,1)S(1)} %add_convert_fusion) | copy-start | bytes 786436
  42.8 14.7 %all-to-all-start.1 = ((bf16[32,32,128]{2,0,1:T(8,128)(2,1)}), bf16[32,32,128]{2,0,1:T(8,128)(2,1)S(1)}, u32[]{:S(2)}, u32[]{:S(2)}) async-start(bf16[32,32,128]{2,0,1:T(8,128)(2,1)} %copy.71), calls=%async_computation.1 | async-start | bytes 524288 | tf_op jit(solution)/shard_map/all_to_all | solution.py:113
  49.3 13.9 %copy-start.14 = (bf16[16,32,1,128]{3,1,0,2:T(8,128)(2,1)}, bf16[16,32,1,128]{3,1,0,2:T(8,128)(2,1)S(1)}, u32[]{:S(2)}) copy-start(bf16[16,32,1,128]{3,1,0,2:T(8,128)(2,1)S(1)} %get-tuple-element.124) | copy-start | bytes 393220
  57.5 5.7 %copy-start.8 = (bf16[32,32,128]{2,0,1:T(8,128)(2,1)}, bf16[32,32,128]{2,0,1:T(8,128)(2,1)S(1)}, u32[]{:S(2)}) copy-start(bf16[32,32,128]{2,0,1:T(8,128)(2,1)S(1)} %all-to-all-done.1) | copy-start | bytes 786436
  57.5 12.8 %all-to-all-start.3 = ((bf16[32,32,128]{2,0,1:T(8,128)(2,1)}), bf16[32,32,128]{2,0,1:T(8,128)(2,1)S(1)}, u32[]{:S(2)}, u32[]{:S(2)}) async-start(bf16[32,32,128]{2,0,1:T(8,128)(2,1)} %copy.73), calls=%async_computation.3 | async-start | bytes 524288 | tf_op jit(solution)/shard_map/all_to_all | solution.py:114
  70.4 13.5 %all-to-all-start.2 = ((bf16[32,32,128]{2,0,1:T(8,128)(2,1)}), bf16[32,32,128]{2,0,1:T(8,128)(2,1)}, u32[]{:S(2)}, u32[]{:S(2)}) async-start(bf16[32,32,128]{2,0,1:T(8,128)(2,1)} %copy_bitcast_fusion), calls=%async_computation.2 | async-start | bytes 524288 | tf_op jit(solution)/shard_map/all_to_all | solution.py:115
  74.8 2.1 copy-start.1
  83.9 3.3 %copy-start.18 = (bf16[16,32,1,128]{3,1,0,2:T(8,128)(2,1)S(1)}, bf16[16,32,1,128]{3,1,0,2:T(8,128)(2,1)}, u32[]{:S(2)}) copy-start(bf16[16,32,1,128]{3,1,0,2:T(8,128)(2,1)} %slice.139) | copy-start | bytes 393220
  85.0 3.4 %copy-start.10 = (bf16[1024,1,128]{2,0,1:T(8,128)(2,1)}, bf16[1024,1,128]{2,0,1:T(8,128)(2,1)S(1)}, u32[]{:S(2)}) copy-start(bf16[1024,1,128]{2,0,1:T(8,128)(2,1)S(1)} %fusion.21) | copy-start | bytes 786436
  87.2 1.8 copy-start.2
  87.5 0.8 copy-start.6
  87.6 1.9 copy-start.9
  89.0 1.6 copy-start.15
  89.5 7.4 %copy-start.7 = (bf16[512,512]{0,1:T(8,128)(2,1)S(1)}, bf16[512,512]{0,1:T(8,128)(2,1)}, u32[]{:S(2)}) copy-start(bf16[512,512]{0,1:T(8,128)(2,1)} %copy-done.6) | copy-start | bytes 1572868
  89.5 7.4 %copy-start.13 = (bf16[16,32,1,128]{3,1,0,2:T(8,128)(2,1)S(1)}, bf16[16,32,1,128]{3,1,0,2:T(8,128)(2,1)}, u32[]{:S(2)}) copy-start(bf16[16,32,1,128]{3,1,0,2:T(8,128)(2,1)} %slice.137) | copy-start | bytes 393220
  92.4 17.3 %copy-start.12 = (bf16[512,128]{1,0:T(8,128)(2,1)S(1)}, bf16[512,128]{1,0:T(8,128)(2,1)}, u32[]{:S(2)}) copy-start(bf16[512,128]{1,0:T(8,128)(2,1)} %convolution_convert_fusion.1) | copy-start | bytes 393220
  93.2 12.8 %all-to-all-start.5 = ((bf16[32,2,2048]{2,1,0:T(2,128)(2,1)}), bf16[32,2,2048]{2,1,0:T(2,128)(2,1)S(1)}, u32[]{:S(2)}, u32[]{:S(2)}) async-start(bf16[32,2,2048]{2,1,0:T(2,128)(2,1)} %reshape.259), calls=%async_computation.5 | async-start | bytes 524288 | tf_op jit(solution)/shard_map/all_to_all | solution.py:140
  97.3 25.9 %copy-start.5 = (bf16[512,512]{0,1:T(8,128)(2,1)S(1)}, bf16[512,512]{0,1:T(8,128)(2,1)}, u32[]{:S(2)}) copy-start(bf16[512,512]{0,1:T(8,128)(2,1)} %fusion.24) | copy-start | bytes 1572868
  97.3 25.9 %copy-start.11 = (bf16[1024,1,128]{2,0,1:T(8,128)(2,1)S(1)}, bf16[1024,1,128]{2,0,1:T(8,128)(2,1)}, u32[]{:S(2)}) copy-start(bf16[1024,1,128]{2,0,1:T(8,128)(2,1)} %copy-done.10) | copy-start | bytes 786436
  106.0 12.8 %all-to-all-start.4 = ((bf16[32,2,2048]{2,1,0:T(2,128)(2,1)}), bf16[32,2,2048]{2,1,0:T(2,128)(2,1)S(1)}, u32[]{:S(2)}, u32[]{:S(2)}) async-start(bf16[32,2,2048]{2,1,0:T(2,128)(2,1)} %reshape.257), calls=%async_computation.4 | async-start | bytes 524288 | tf_op jit(solution)/shard_map/all_to_all | solution.py:137
  118.8 13.5 %all-to-all-start.7 = ((bf16[32,2,2048]{2,1,0:T(2,128)(2,1)}), bf16[32,2,2048]{2,1,0:T(2,128)(2,1)}, u32[]{:S(2)}, u32[]{:S(2)}) async-start(bf16[32,2,2048]{2,1,0:T(2,128)(2,1)} %reshape.263), calls=%async_computation.7 | async-start | bytes 524288 | tf_op jit(solution)/shard_map/all_to_all | solution.py:142
  132.3 91.7 %all-to-all-start.6 = ((bf16[32,2,2048]{2,1,0:T(2,128)(2,1)}), bf16[32,2,2048]{2,1,0:T(2,128)(2,1)}, u32[]{:S(2)}, u32[]{:S(2)}) async-start(bf16[32,2,2048]{2,1,0:T(2,128)(2,1)} %reshape.261), calls=%async_computation.6 | async-start | bytes 524288 | tf_op jit(solution)/shard_map/all_to_all | solution.py:141
  138.5 4.0 %copy-start.4 = (bf16[32,4096]{1,0:T(8,128)(2,1)S(1)}, bf16[32,4096]{1,0:T(8,128)(2,1)}, u32[]{:S(2)}) copy-start(bf16[32,4096]{1,0:T(8,128)(2,1)} %copy-done.3) | copy-start | bytes 786436
where the time goes:
time: 229 us; the launch traced here: 227 us
  blocking collectives  104 us (45%)
  starting transfers between devices  41 us (18%)
  waiting for transfers between devices  31.5 us (14%)
  local copies, waits for them, and re-layouts  22 us (10%)
  other arithmetic  15 us (7%)
  matrix products  11.5 us (5%)
    psum x1, blocking collectives, per_device(): gain_total = lax.psum(seq_terms, ('grp', 'seq'))  80.6 us
    all_gather x1, blocking collectives, per_device(): all_starts = lax.all_gather(seg_starts[0], 'seq', axis=0, tiled=True)  23.7 us
    unnamed x54, local copies, waits for them, and re-layouts  12.4 us
    all_to_all x1, starting transfers between devices, per_device(): lax.all_to_all(by_heads(queries[0]), 'seq', split_axis=1, concat_axis=0,...  8.59 us
    all_to_all x1, waiting for transfers between devices, per_device(): lax.all_to_all(by_heads(attn_keys[0]), 'seq', split_axis=1, concat_axis=0...  8.21 us
    transpose x6, other arithmetic, per_device(): jnp.moveaxis(operand, 0, 1)  8.13 us
    all_to_all x1, starting transfers between devices, per_device(): lax.all_to_all(by_heads(attn_keys[0]), 'seq', split_axis=1, concat_axis=0...  5.75 us
    all_to_all x1, waiting for transfers between devices, per_device(): lax.all_to_all(by_heads(attn_values[0]), 'seq', split_axis=1, concat_axis...  5.39 us
  transfers between devices with their start and end apart: 9, of which 6 were waited for; matrix products, arithmetic and copies ran while one was open for 15% of the time, Pallas kernels for 0%

commit v1 on v0

--- a/solution.py
+++ b/solution.py
@@ -145,7 +145,7 @@
     )
     seq_out = returned[3].reshape(slot_count, model_width)
     seq_terms = jnp.sum(seq_out.astype(jnp.float32) * pooled_low.astype(jnp.float32), axis=0)
-    gain_total = lax.psum(seq_terms, ("grp", "seq"))
+    gain_total = jnp.sum(lax.all_gather(seq_terms, ("grp", "seq")), axis=0)
     grad_gain = lax.dynamic_slice_in_dim(gain_total, shard_index * col_count, col_count)
     return (to_seq(returned[0]), to_seq(returned[1]), to_seq(returned[2]), grad_gain)
 

time: 229 us -> 246 us (1.074)
  blocking collectives: 104 us -> 35.3 us
  waiting for transfers between devices: 31.5 us -> 98.7 us
  between operations: 1.82 us -> 15.2 us
  local copies, waits for them, and re-layouts: 22 us -> 27.7 us
  starting transfers between devices: 41 us -> 36.8 us
  matrix products: 11.5 us -> 14.2 us
    psum x1 -> x0, blocking collectives: 80.6 us -> none  [per_device(): gain_total = lax.psum(seq_terms, ('grp', 'seq'))]
    all_gather x0 -> x1, waiting for transfers between devices: none -> 67.2 us  [per_device(): gain_total = jnp.sum(lax.all_gather(seq_terms, ('grp', 'seq')), axis=0)]
    all_to_all x0 -> x1, blocking collectives: none -> 13.5 us  [per_device(): lax.all_to_all(shortened(attn_out), 'seq', split_axis=0, concat_axis=1, t...]
    all_to_all x1 -> x0, waiting for transfers between devices: 5.14 us -> none  [per_device(): lax.all_to_all(shortened(attn_out), 'seq', split_axis=0, concat_axis=1, t...]
    all_gather x0 -> x1, local copies, waits for them, and re-layouts: none -> 4.97 us  [per_device(): gain_total = jnp.sum(lax.all_gather(seq_terms, ('grp', 'seq')), axis=0)]
    all_to_all x1, waiting for transfers between devices: 0.01 us -> 4.69 us  [per_device(): lax.all_to_all(grad_value, 'seq', split_axis=0, concat_axis=1, tiled=True)]
    all_to_all x1 -> x0, starting transfers between devices: 4.38 us -> none  [per_device(): lax.all_to_all(shortened(attn_out), 'seq', split_axis=0, concat_axis=1, t...]
    all_to_all x1, starting transfers between devices: 8.59 us -> 5.46 us  [per_device(): lax.all_to_all(by_heads(queries[0]), 'seq', split_axis=1, concat_axis=0,...]
  transfers between devices with their start and end apart: 9 -> 9, of which waited for: 6 -> 7; matrix products, arithmetic and copies ran while one was open for 15% -> 14% of each run, Pallas kernels for 0% -> 0%
where the time goes in v1:
time: 246 us; the launch traced here: 245 us
  waiting for transfers between devices  98.7 us (40%)
  starting transfers between devices  36.8 us (15%)
  blocking collectives  35.3 us (14%)
  local copies, waits for them, and re-layouts  27.7 us (11%)
  other arithmetic  17 us (7%)
  between operations  15.2 us (6%)
  matrix products  14.2 us (6%)
    all_gather x1, waiting for transfers between devices, per_device(): gain_total = jnp.sum(lax.all_gather(seq_terms, ('grp', 'seq')), axis=0)  67.2 us
    all_gather x1, blocking collectives, per_device(): all_starts = lax.all_gather(seg_starts[0], 'seq', axis=0, tiled=True)  21.8 us
    all_to_all x1, blocking collectives, per_device(): lax.all_to_all(shortened(attn_out), 'seq', split_axis=0, concat_axis=1, t...  13.5 us
    unnamed x52, local copies, waits for them, and re-layouts  13.1 us
    all_to_all x1, waiting for transfers between devices, per_device(): lax.all_to_all(by_heads(attn_keys[0]), 'seq', split_axis=1, concat_axis=0...  8.51 us
    all_to_all x1, waiting for transfers between devices, per_device(): lax.all_to_all(by_heads(attn_values[0]), 'seq', split_axis=1, concat_axis...  7.67 us
    transpose x6, other arithmetic, per_device(): jnp.moveaxis(operand, 0, 1)  7.2 us
    all_to_all x1, starting transfers between devices, per_device(): lax.all_to_all(by_heads(attn_keys[0]), 'seq', split_axis=1, concat_axis=0...  5.46 us
  transfers between devices with their start and end apart: 9, of which 7 were waited for; matrix products, arithmetic and copies ran while one was open for 14% of the time, Pallas kernels for 0%

profile of v1, /device:TPU:1, one launch (start us, length us, event | category | flops | bytes accessed | tf_op | source)
XLA Modules:
  0.0 244.8 jit_solution(1408164344348196173)
XLA Ops:
  7.2 0.9 convert_reduce_fusion
  9.2 5.1 %collective-permute-start = (f32[1,4096]{1,0:T(1,128)S(1)}, f32[1,4096]{1,0:T(1,128)S(1)}, u32[]{:S(2)}, u32[]{:S(2)}) collective-permute-start(f32[1,4096]{1,0:T(1,128)S(1)} %fusion), channel_id=1, source_target_pairs={{1,0},{2,1},{3,2},{4,3},{5,4},{6,5},{7,6},{8,7},{9,8},{10,9},{11,1... | collective-permute-start | bytes 49160 | tf_op jit(solution)/shard_map/ppermute | solution.py:13
  14.5 0.8 copy.70
  15.3 5.5 %all-to-all-start = ((bf16[32,32,128]{2,0,1:T(8,128)(2,1)}), bf16[32,32,128]{2,0,1:T(8,128)(2,1)S(1)}, u32[]{:S(2)}, u32[]{:S(2)}) async-start(bf16[32,32,128]{2,0,1:T(8,128)(2,1)} %copy.70), calls=%async_computation | async-start | bytes 524288 | tf_op jit(solution)/shard_map/all_to_all | solution.py:112
  21.4 21.8 %all-gather = s32[32,1,32]{2,1,0:T(1,128)S(1)} all-gather(s32[1,1,32]{2,1,0:T(1,128)S(1)} %copy-done.18), channel_id=2, replica_groups=mesh['grp'=8,'seq'=32] {'seq'}, dimensions={0}, use_global_device_ids=true | all-gather | bytes 4224 | tf_op jit(solution)/shard_map/all_gather | solution.py:104
  44.2 0.8 copy.71
  45.0 0.8 copy.73
  46.6 5.5 %all-to-all-start.1 = ((bf16[32,32,128]{2,0,1:T(8,128)(2,1)}), bf16[32,32,128]{2,0,1:T(8,128)(2,1)S(1)}, u32[]{:S(2)}, u32[]{:S(2)}) async-start(bf16[32,32,128]{2,0,1:T(8,128)(2,1)} %copy.71), calls=%async_computation.1 | async-start | bytes 524288 | tf_op jit(solution)/shard_map/all_to_all | solution.py:113
  52.5 8.5 %all-to-all-done.1 = bf16[32,32,128]{2,0,1:T(8,128)(2,1)S(1)} async-done(((bf16[32,32,128]{2,0,1:T(8,128)(2,1)}), bf16[32,32,128]{2,0,1:T(8,128)(2,1)S(1)}, u32[]{:S(2)}, u32[]{:S(2)}) %all-to-all-start.1) | async-done | bytes 262176 | tf_op jit(solution)/shard_map/all_to_all | solution.py:113
  61.1 3.7 %all-to-all-start.3 = ((bf16[32,32,128]{2,0,1:T(8,128)(2,1)}), bf16[32,32,128]{2,0,1:T(8,128)(2,1)S(1)}, u32[]{:S(2)}, u32[]{:S(2)}) async-start(bf16[32,32,128]{2,0,1:T(8,128)(2,1)} %copy.73), calls=%async_computation.3 | async-start | bytes 524288 | tf_op jit(solution)/shard_map/all_to_all | solution.py:114
  66.2 7.7 %all-to-all-done.3 = bf16[32,32,128]{2,0,1:T(8,128)(2,1)S(1)} async-done(((bf16[32,32,128]{2,0,1:T(8,128)(2,1)}), bf16[32,32,128]{2,0,1:T(8,128)(2,1)S(1)}, u32[]{:S(2)}, u32[]{:S(2)}) %all-to-all-start.3) | async-done | bytes 262176 | tf_op jit(solution)/shard_map/all_to_all | solution.py:114
  73.9 4.4 %all-to-all-start.2 = ((bf16[32,32,128]{2,0,1:T(8,128)(2,1)}), bf16[32,32,128]{2,0,1:T(8,128)(2,1)}, u32[]{:S(2)}, u32[]{:S(2)}) async-start(bf16[32,32,128]{2,0,1:T(8,128)(2,1)} %copy_bitcast_fusion), calls=%async_computation.2 | async-start | bytes 524288 | tf_op jit(solution)/shard_map/all_to_all | solution.py:115
  79.0 0.8 fusion.32
  81.7 1.1 convolution_convert_fusion.1
  82.8 1.0 fusion.24
  83.8 3.6 %all-to-all-done.2 = bf16[32,32,128]{2,0,1:T(8,128)(2,1)} async-done(((bf16[32,32,128]{2,0,1:T(8,128)(2,1)}), bf16[32,32,128]{2,0,1:T(8,128)(2,1)}, u32[]{:S(2)}, u32[]{:S(2)}) %all-to-all-start.2) | async-done | bytes 262176 | tf_op jit(solution)/shard_map/all_to_all | solution.py:115
  87.4 1.0 bitcast_convert_fusion
  89.2 1.6 multiply_reduce_fusion.1
  92.0 2.4 reduce.19
  94.4 1.7 reshape.264
  96.1 13.5 %all_to_all.108 = bf16[32,2,2048]{2,1,0:T(2,128)(2,1)} all-to-all(bf16[32,2,2048]{2,1,0:T(2,128)(2,1)} %reshape.264), channel_id=1, replica_groups=mesh['grp'=8,'seq'=32] {'seq'}, dimensions={0} | all-to-all | bytes 524288 | tf_op jit(solution)/shard_map/all_to_all | solution.py:142
  109.6 2.8 %reshape.265 = bf16[1024,1,128]{2,1,0:T(2,128)(2,1)} reshape(bf16[32,2,2048]{2,1,0:T(2,128)(2,1)} %all_to_all.108) | data formatting | bytes 524288
  112.4 1.6 convert_element_type.145
  114.4 0.9 fusion.20
  115.4 1.4 fusion.9
  118.6 1.5 reduce.16
  120.1 1.7 reshape.258
  121.8 4.6 %all-to-all-start.4 = ((bf16[32,2,2048]{2,1,0:T(2,128)(2,1)}), bf16[32,2,2048]{2,1,0:T(2,128)(2,1)}, u32[]{:S(2)}, u32[]{:S(2)}) async-start(bf16[32,2,2048]{2,1,0:T(2,128)(2,1)} %reshape.258), calls=%async_computation.4 | async-start | bytes 524288 | tf_op jit(solution)/shard_map/all_to_all | solution.py:137
  126.4 1.4 fusion.34
  127.7 2.1 fusion.13
  129.8 1.8 reduce.17
  131.6 0.8 reshape.260
  132.4 3.0 %all-to-all-done.4 = bf16[32,2,2048]{2,1,0:T(2,128)(2,1)} async-done(((bf16[32,2,2048]{2,1,0:T(2,128)(2,1)}), bf16[32,2,2048]{2,1,0:T(2,128)(2,1)}, u32[]{:S(2)}, u32[]{:S(2)}) %all-to-all-start.4) | async-done | bytes 262176 | tf_op jit(solution)/shard_map/all_to_all | solution.py:137
  135.4 4.3 %all-to-all-start.5 = ((bf16[32,2,2048]{2,1,0:T(2,128)(2,1)}), bf16[32,2,2048]{2,1,0:T(2,128)(2,1)S(1)}, u32[]{:S(2)}, u32[]{:S(2)}) async-start(bf16[32,2,2048]{2,1,0:T(2,128)(2,1)} %reshape.260), calls=%async_computation.5 | async-start | bytes 524288 | tf_op jit(solution)/shard_map/all_to_all | solution.py:140
  139.7 1.3 fusion.25
  141.0 2.1 fusion.14
  143.1 0.8 reduce.18
  144.0 0.8 reshape.262
  144.7 4.0 %all-to-all-done.5 = bf16[32,2,2048]{2,1,0:T(2,128)(2,1)S(1)} async-done(((bf16[32,2,2048]{2,1,0:T(2,128)(2,1)}), bf16[32,2,2048]{2,1,0:T(2,128)(2,1)S(1)}, u32[]{:S(2)}, u32[]{:S(2)}) %all-to-all-start.5) | async-done | bytes 262176 | tf_op jit(solution)/shard_map/all_to_all | solution.py:140
  148.7 3.7 %all-to-all-start.6 = ((bf16[32,2,2048]{2,1,0:T(2,128)(2,1)}), bf16[32,2,2048]{2,1,0:T(2,128)(2,1)S(1)}, u32[]{:S(2)}, u32[]{:S(2)}) async-start(bf16[32,2,2048]{2,1,0:T(2,128)(2,1)} %reshape.262), calls=%async_computation.6 | async-start | bytes 524288 | tf_op jit(solution)/shard_map/all_to_all | solution.py:141
  152.9 0.8 reshape.241
  153.7 2.2 reshape.259
  156.0 0.8 reshape.240
  156.8 4.7 %all-to-all-done.6 = bf16[32,2,2048]{2,1,0:T(2,128)(2,1)S(1)} async-done(((bf16[32,2,2048]{2,1,0:T(2,128)(2,1)}), bf16[32,2,2048]{2,1,0:T(2,128)(2,1)S(1)}, u32[]{:S(2)}, u32[]{:S(2)}) %all-to-all-start.6) | async-done | bytes 262176 | tf_op jit(solution)/shard_map/all_to_all | solution.py:141
  161.9 0.8 reshape.242
  162.8 67.2 %all-gather.4.cloned.1.call-done = f32[1048576]{0:T(1024)} async-done(((f32[4096]{0:T(1024)}), f32[1048576]{0:T(1024)}) %all-gather.4.cloned.1.call-update) | async-done | bytes 4194320 | tf_op jit(solution)/shard_map/all_gather | solution.py:148
  230.0 5.0 %reshape.248 = f32[256,4096]{1,0:T(8,128)} reshape(f32[1048576]{0:T(1024)} %all-gather.4.cloned.1.call-done) | data formatting | bytes 8388608 | tf_op jit(solution)/shard_map/all_gather | solution.py:148
  234.9 2.4 reduce_sum.83
  (83 shorter events, 13.1 us)
Async XLA Ops:
  7.2 1.7 copy-start
  7.2 13.6 %copy-start.18 = (s32[1,1,32]{2,1,0:T(1,128)S(1)}, s32[1,1,32]{2,1,0:T(1,128)}, u32[]{:S(2)}) copy-start(s32[1,1,32]{2,1,0:T(1,128)} %param.22) | copy-start | bytes 388
  7.2 7.2 %copy-start.15 = (bf16[1,32,4096]{2,1,0:T(8,128)(2,1)S(1)}, bf16[1,32,4096]{2,1,0:T(8,128)(2,1)}, u32[]{:S(2)}) copy-start(bf16[1,32,4096]{2,1,0:T(8,128)(2,1)} %param.18) | copy-start | bytes 786436
  7.2 36.9 %copy-start.16 = (bf16[1,32,4096]{2,1,0:T(8,128)(2,1)S(1)}, bf16[1,32,4096]{2,1,0:T(8,128)(2,1)}, u32[]{:S(2)}) copy-start(bf16[1,32,4096]{2,1,0:T(8,128)(2,1)} %param.19) | copy-start | bytes 786436
  8.9 36.1 %copy-start.17 = (bf16[1,32,4096]{2,1,0:T(8,128)(2,1)S(1)}, bf16[1,32,4096]{2,1,0:T(8,128)(2,1)}, u32[]{:S(2)}) copy-start(bf16[1,32,4096]{2,1,0:T(8,128)(2,1)} %param.20) | copy-start | bytes 786436
  9.2 42.8 %collective-permute-start = (f32[1,4096]{1,0:T(1,128)S(1)}, f32[1,4096]{1,0:T(1,128)S(1)}, u32[]{:S(2)}, u32[]{:S(2)}) collective-permute-start(f32[1,4096]{1,0:T(1,128)S(1)} %fusion), channel_id=1, source_target_pairs={{1,0},{2,1},{3,2},{4,3},{5,4},{6,5},{7,6},{8,7},{9,8},{10,9},{11,1... | collective-permute-start | bytes 49160 | tf_op jit(solution)/shard_map/ppermute | solution.py:13
  15.3 31.3 %all-to-all-start = ((bf16[32,32,128]{2,0,1:T(8,128)(2,1)}), bf16[32,32,128]{2,0,1:T(8,128)(2,1)S(1)}, u32[]{:S(2)}, u32[]{:S(2)}) async-start(bf16[32,32,128]{2,0,1:T(8,128)(2,1)} %copy.70), calls=%async_computation | async-start | bytes 524288 | tf_op jit(solution)/shard_map/all_to_all | solution.py:112
  46.6 14.5 %all-to-all-start.1 = ((bf16[32,32,128]{2,0,1:T(8,128)(2,1)}), bf16[32,32,128]{2,0,1:T(8,128)(2,1)S(1)}, u32[]{:S(2)}, u32[]{:S(2)}) async-start(bf16[32,32,128]{2,0,1:T(8,128)(2,1)} %copy.71), calls=%async_computation.1 | async-start | bytes 524288 | tf_op jit(solution)/shard_map/all_to_all | solution.py:113
  52.5 27.2 %copy-start.3 = (bf16[32,4096]{1,0:T(8,128)(2,1)}, bf16[32,4096]{1,0:T(8,128)(2,1)S(1)}, u32[]{:S(2)}) copy-start(bf16[32,4096]{1,0:T(8,128)(2,1)S(1)} %add_convert_fusion) | copy-start | bytes 786436
  61.0 18.7 %copy-start.6 = (bf16[32,32,128]{2,0,1:T(8,128)(2,1)}, bf16[32,32,128]{2,0,1:T(8,128)(2,1)S(1)}, u32[]{:S(2)}) copy-start(bf16[32,32,128]{2,0,1:T(8,128)(2,1)S(1)} %all-to-all-done.1) | copy-start | bytes 786436
  61.1 12.8 %all-to-all-start.3 = ((bf16[32,32,128]{2,0,1:T(8,128)(2,1)}), bf16[32,32,128]{2,0,1:T(8,128)(2,1)S(1)}, u32[]{:S(2)}, u32[]{:S(2)}) async-start(bf16[32,32,128]{2,0,1:T(8,128)(2,1)} %copy.73), calls=%async_computation.3 | async-start | bytes 524288 | tf_op jit(solution)/shard_map/all_to_all | solution.py:114
  66.2 14.1 %copy-start.14 = (bf16[16,32,1,128]{3,1,0,2:T(8,128)(2,1)}, bf16[16,32,1,128]{3,1,0,2:T(8,128)(2,1)S(1)}, u32[]{:S(2)}) copy-start(bf16[16,32,1,128]{3,1,0,2:T(8,128)(2,1)S(1)} %get-tuple-element.124) | copy-start | bytes 393220
  73.9 13.5 %all-to-all-start.2 = ((bf16[32,32,128]{2,0,1:T(8,128)(2,1)}), bf16[32,32,128]{2,0,1:T(8,128)(2,1)}, u32[]{:S(2)}, u32[]{:S(2)}) async-start(bf16[32,32,128]{2,0,1:T(8,128)(2,1)} %copy_bitcast_fusion), calls=%async_computation.2 | async-start | bytes 524288 | tf_op jit(solution)/shard_map/all_to_all | solution.py:115
  78.3 151.7 %all-gather.4.cloned.1.call-start = ((), (), s32[]{:S(2)}) async-start(), calls=%async_computation.8 | async-start | bytes 4210688 | tf_op jit(solution)/shard_map/all_gather | solution.py:148
  80.3 0.9 copy-start.12
  80.8 2.1 copy-start.1
  87.4 3.4 %copy-start.11 = (bf16[512,128]{1,0:T(8,128)(2,1)S(1)}, bf16[512,128]{1,0:T(8,128)(2,1)}, u32[]{:S(2)}) copy-start(bf16[512,128]{1,0:T(8,128)(2,1)} %convolution_convert_fusion.1) | copy-start | bytes 393220
  88.5 0.7 copy-start.8
  112.4 1.9 copy-start.4
  115.3 1.5 copy-start.13
  115.3 2.3 copy-start.2
  115.3 2.3 copy-start.9
  116.8 0.8 copy-start.5
  116.8 1.3 copy-start.7
  121.8 13.6 %all-to-all-start.4 = ((bf16[32,2,2048]{2,1,0:T(2,128)(2,1)}), bf16[32,2,2048]{2,1,0:T(2,128)(2,1)}, u32[]{:S(2)}, u32[]{:S(2)}) async-start(bf16[32,2,2048]{2,1,0:T(2,128)(2,1)} %reshape.258), calls=%async_computation.4 | async-start | bytes 524288 | tf_op jit(solution)/shard_map/all_to_all | solution.py:137
  126.3 13.3 %copy-start.10 = (bf16[1024,1,128]{2,0,1:T(8,128)(2,1)S(1)}, bf16[1024,1,128]{2,0,1:T(8,128)(2,1)}, u32[]{:S(2)}) copy-start(bf16[1024,1,128]{2,0,1:T(8,128)(2,1)} %copy-done.8) | copy-start | bytes 786436
  135.4 13.3 %all-to-all-start.5 = ((bf16[32,2,2048]{2,1,0:T(2,128)(2,1)}), bf16[32,2,2048]{2,1,0:T(2,128)(2,1)S(1)}, u32[]{:S(2)}, u32[]{:S(2)}) async-start(bf16[32,2,2048]{2,1,0:T(2,128)(2,1)} %reshape.260), calls=%async_computation.5 | async-start | bytes 524288 | tf_op jit(solution)/shard_map/all_to_all | solution.py:140
  148.7 12.8 %all-to-all-start.6 = ((bf16[32,2,2048]{2,1,0:T(2,128)(2,1)}), bf16[32,2,2048]{2,1,0:T(2,128)(2,1)S(1)}, u32[]{:S(2)}, u32[]{:S(2)}) async-start(bf16[32,2,2048]{2,1,0:T(2,128)(2,1)} %reshape.262), calls=%async_computation.6 | async-start | bytes 524288 | tf_op jit(solution)/shard_map/all_to_all | solution.py:141
Sparse Core Ops, SparseCore 0:
  115.4 114.4 all-gather.3
